TPU v7x, 32 devices: a whole 2x2x4 slice. The times are simulated.
32 devices in a mesh: shard: 8 (over y, x, core), rep: 4 (over z).
Axes of the slice: x: 2, y: 2, z: 4, core: 2. Of those that a mesh axis runs over, the one named last changes fastest.
Arguments:
- tokens: bfloat16 [16384, 1472], P(('shard', 'rep')), may hold values from -6 to 6
- cotangent: bfloat16 [16384, 1472], P(('shard', 'rep')), may hold values from -6 to 6
- buckets: int32 [1023], replicated, may hold values from 0 to 31
- bias_table: bfloat16 [32, 6], replicated, may hold values from -4 to 4
- attn_gain: bfloat16 [1472], P('shard'), may hold values from 0.25 to 1.75
- w_query: bfloat16 [1472, 384], P('shard'), may hold values from -0.0390625 to 0.0390625
- w_key: bfloat16 [1472, 384], P('shard'), may hold values from -0.15625 to 0.15625
- w_value: bfloat16 [1472, 384], P('shard'), may hold values from -0.15625 to 0.15625
- w_output: bfloat16 [1472, 384], P('shard'), may hold values from -1.25 to 1.25
- ffn_gain: bfloat16 [1472], P('shard'), may hold values from 0.25 to 1.75
- w_gate: bfloat16 [1472, 3584], P('shard'), may hold values from -0.15625 to 0.15625
- w_up: bfloat16 [1472, 3584], P('shard'), may hold values from -0.15625 to 0.15625
- w_down: bfloat16 [1472, 3584], P('shard'), may hold values from -0.09375 to 0.09375
Outputs:
- layer_out: bfloat16 [16384, 1472], P(('shard', 'rep'))
- grad_tokens: bfloat16 [16384, 1472], P(('shard', 'rep'))
- grad_attn_gain: float32 [1472], P('shard')
- grad_w_query: float32 [1472, 384], P('shard')
- grad_w_key: float32 [1472, 384], P('shard')
- grad_w_value: float32 [1472, 384], P('shard')
- grad_w_output: float32 [1472, 384], P('shard')
- grad_ffn_gain: float32 [1472], P('shard')
- grad_w_gate: float32 [1472, 3584], P('shard')
- grad_w_up: float32 [1472, 3584], P('shard')
- grad_w_down: float32 [1472, 3584], P('shard')
- grad_bias_table: float32 [32, 6], replicated
All inputs are finite; a program needn't handle non-finite values.
Results may differ from a plain program's by a relative error of at most 0.015.
The roundings to bfloat16 on the way count: a program that leaves them out, or rounds other values in their place, can miss the bound.
Values may be sent and summed in bfloat16 or wider, within the bound.
A program may use at most 320 MiB of HBM per device.

v0:
```python
import jax
import jax.numpy as jnp
from jax import lax
from jax.sharding import PartitionSpec as P

BLOCK = 256


norm_eps = 1e-06
masked_score = -1e30
highest = lax.Precision.HIGHEST


def norm_local(row_values, gain_vector):
    return (
        row_values
        * lax.rsqrt(jnp.mean(row_values * row_values, axis=-1, keepdims=True) + norm_eps)
        * gain_vector
    )


def gelu_tanh(values_in):
    return jax.nn.gelu(values_in, approximate=True)


def diagonal_total(matrix):
    head_count, row_count, key_count = matrix.shape
    flipped = matrix[:, :, ::-1]
    padded = jnp.concatenate(
        [flipped, jnp.zeros((head_count, row_count, row_count), jnp.float32)], axis=2
    )
    flat_rows = padded.reshape(head_count, row_count * (key_count + row_count))
    flat_rows = flat_rows[:, : row_count * (key_count + row_count - 1)]
    return jnp.sum(flat_rows.reshape(head_count, row_count, key_count + row_count - 1), axis=1)


def toeplitz_grid(offset_bias, row_count, length):
    head_count = offset_bias.shape[0]
    span = length + row_count - 1
    flipped = offset_bias[:, ::-1]
    rotated = jnp.concatenate([flipped[:, row_count - 1 :], flipped[:, : row_count - 1]], axis=1)
    tiled = jnp.tile(rotated, (1, row_count))[:, : row_count * (span - 1)]
    return tiled.reshape(head_count, row_count, span - 1)[:, :, :length]


def body(
    tokens,
    cotangent,
    buckets,
    bias_table,
    attn_gain,
    w_query,
    w_key,
    w_value,
    w_output,
    ffn_gain,
    w_gate,
    w_up,
    w_down,
):
    length = tokens.shape[0]
    bucket_count = bias_table.shape[0]
    head_count = bias_table.shape[1]
    inner_width = w_query.shape[1]
    ff_width = w_gate.shape[1]
    owner_rows = w_query.shape[0]
    head_size = inner_width // head_count
    block_rows = min(512, length)
    block_count = length // block_rows
    residual = tokens.astype(jnp.float32)
    attn_set = (
        lax.all_gather(attn_gain, "shard", axis=0, tiled=True),
        lax.all_gather(w_query, "shard", axis=0, tiled=True),
        lax.all_gather(w_key, "shard", axis=0, tiled=True),
        lax.all_gather(w_value, "shard", axis=0, tiled=True),
        lax.all_gather(w_output, "shard", axis=0, tiled=True),
    )
    gain_one = attn_set[0].astype(jnp.float32)
    normed_one = norm_local(residual, gain_one).astype(jnp.bfloat16)

    def project(weight):
        product = jnp.dot(normed_one, weight, preferred_element_type=jnp.float32)
        return product.astype(jnp.bfloat16).reshape(length, head_count, head_size)

    queries = project(attn_set[1])
    key_rows = project(attn_set[2])
    value_rows = project(attn_set[3])
    one_hot = (buckets[:, None] == jnp.arange(bucket_count, dtype=jnp.int32)[None, :]).astype(
        jnp.float32
    )
    offset_bias = jnp.dot(one_hot, bias_table.astype(jnp.float32), precision=highest).T
    block_starts = jnp.arange(block_count, dtype=jnp.int32) * block_rows
    key_index = jnp.arange(length, dtype=jnp.int32)

    def block_scores(first_row, query_block):
        query_index = first_row + jnp.arange(block_rows, dtype=jnp.int32)
        bias_grid = toeplitz_grid(offset_bias, block_rows, length)
        scores = (
            jnp.einsum("qhd,khd->hqk", query_block, key_rows, preferred_element_type=jnp.float32)
            + bias_grid
        )
        allowed = key_index[None, :] // BLOCK <= query_index[:, None] // BLOCK
        return jnp.where(allowed[None], scores, masked_score)

    def attend(first_row):
        scores = block_scores(first_row, queries)
        row_max = jnp.max(scores, axis=-1, keepdims=True)
        exp_scores = jnp.exp(scores - row_max)
        totals = jnp.sum(exp_scores, axis=-1, keepdims=True)
        probability = (exp_scores / totals).astype(jnp.bfloat16)
        mixed_rows = jnp.einsum(
            "hqk,khd->qhd", probability, value_rows, preferred_element_type=jnp.float32
        )
        return (mixed_rows, (row_max + jnp.log(totals))[..., 0])

    mixed_blocks, log_totals = lax.map(attend, block_starts)
    attended = mixed_blocks.reshape(length, inner_width).astype(jnp.bfloat16)
    middle = residual + jnp.einsum(
        "ti,di->td", attended, attn_set[4], preferred_element_type=jnp.float32
    )
    ffn_set = (
        lax.all_gather(ffn_gain, "shard", axis=0, tiled=True),
        lax.all_gather(w_gate, "shard", axis=0, tiled=True),
        lax.all_gather(w_up, "shard", axis=0, tiled=True),
        lax.all_gather(w_down, "shard", axis=0, tiled=True),
    )
    gain_two = ffn_set[0].astype(jnp.float32)
    normed_two = norm_local(middle, gain_two).astype(jnp.bfloat16)
    gate_values = jnp.dot(normed_two, ffn_set[1], preferred_element_type=jnp.float32)
    up_values = jnp.dot(normed_two, ffn_set[2], preferred_element_type=jnp.float32)
    activated, gelu_pullback = jax.vjp(gelu_tanh, gate_values)
    hidden = (activated * up_values).astype(jnp.bfloat16)
    layer_out = (
        middle + jnp.einsum("tf,df->td", hidden, ffn_set[3], preferred_element_type=jnp.float32)
    ).astype(jnp.bfloat16)
    ffn_set = (
        lax.all_gather(ffn_gain, "shard", axis=0, tiled=True),
        lax.all_gather(w_gate, "shard", axis=0, tiled=True),
        lax.all_gather(w_up, "shard", axis=0, tiled=True),
        lax.all_gather(w_down, "shard", axis=0, tiled=True),
    )
    grad_w_down = jnp.einsum("td,tf->df", cotangent, hidden, preferred_element_type=jnp.float32)
    grad_hidden = jnp.dot(cotangent, ffn_set[3], preferred_element_type=jnp.float32)
    grad_gate = gelu_pullback(grad_hidden * up_values)[0].astype(jnp.bfloat16)
    grad_up = (grad_hidden * activated).astype(jnp.bfloat16)
    grad_w_gate = jnp.einsum("td,tf->df", normed_two, grad_gate, preferred_element_type=jnp.float32)
    grad_w_up = jnp.einsum("td,tf->df", normed_two, grad_up, preferred_element_type=jnp.float32)
    grad_normed_two = jnp.einsum(
        "tf,df->td", grad_gate, ffn_set[1], preferred_element_type=jnp.float32
    )
    grad_normed_two = grad_normed_two + jnp.einsum(
        "tf,df->td", grad_up, ffn_set[2], preferred_element_type=jnp.float32
    )
    middle_part, grad_gain_two = jax.vjp(norm_local, middle, gain_two)[1](grad_normed_two)
    grad_middle = cotangent.astype(jnp.float32) + middle_part
    ffn_shards = (
        lax.psum_scatter(grad_w_gate.reshape(-1), "shard", scatter_dimension=0, tiled=True),
        lax.psum_scatter(grad_w_up.reshape(-1), "shard", scatter_dimension=0, tiled=True),
        lax.psum_scatter(grad_w_down.reshape(-1), "shard", scatter_dimension=0, tiled=True),
    )
    attn_set = (
        lax.all_gather(attn_gain, "shard", axis=0, tiled=True),
        lax.all_gather(w_query, "shard", axis=0, tiled=True),
        lax.all_gather(w_key, "shard", axis=0, tiled=True),
        lax.all_gather(w_value, "shard", axis=0, tiled=True),
        lax.all_gather(w_output, "shard", axis=0, tiled=True),
    )
    grad_branch = grad_middle.astype(jnp.bfloat16)
    grad_w_output = jnp.einsum(
        "td,ti->di", grad_branch, attended, preferred_element_type=jnp.float32
    )
    grad_attended = jnp.einsum(
        "td,di->ti", grad_branch, attn_set[4], preferred_element_type=jnp.float32
    )
    grad_attended = grad_attended.astype(jnp.bfloat16).reshape(length, head_count, head_size)

    def attend_back(carried, block_input):
        grad_keys, grad_values, grad_offsets = carried
        first_row, log_total = block_input
        scores = block_scores(first_row, queries)
        probability = jnp.exp(scores - log_total[..., None])
        grad_probs = jnp.einsum(
            "qhd,khd->hqk", grad_attended, value_rows, preferred_element_type=jnp.float32
        )
        inner_sum = jnp.sum(probability * grad_probs, axis=-1, keepdims=True)
        grad_scores = (probability * (grad_probs - inner_sum)).astype(jnp.bfloat16)
        grad_values = grad_values + jnp.einsum(
            "hqk,qhd->khd",
            probability.astype(jnp.bfloat16),
            grad_attended,
            preferred_element_type=jnp.float32,
        )
        grad_keys = grad_keys + jnp.einsum(
            "hqk,qhd->khd", grad_scores, queries, preferred_element_type=jnp.float32
        )
        grad_queries = jnp.einsum(
            "hqk,khd->qhd", grad_scores, key_rows, preferred_element_type=jnp.float32
        )
        diagonal_sums = diagonal_total(grad_scores.astype(jnp.float32))
        offset_piece = grad_offsets
        grad_offsets = offset_piece + diagonal_sums
        return ((grad_keys, grad_values, grad_offsets), grad_queries)

    zero_rows = jnp.zeros((length, head_count, head_size), jnp.float32)
    zero_offsets = jnp.zeros((head_count, 2 * length - 1), jnp.float32)
    (grad_keys, grad_values, grad_offsets), query_blocks = lax.scan(
        attend_back, (zero_rows, zero_rows, zero_offsets), (block_starts, log_totals)
    )
    grad_queries = query_blocks.reshape(length, inner_width).astype(jnp.bfloat16)
    grad_keys = grad_keys.reshape(length, inner_width).astype(jnp.bfloat16)
    grad_values = grad_values.reshape(length, inner_width).astype(jnp.bfloat16)
    grad_w_query = jnp.einsum(
        "td,ti->di", normed_one, grad_queries, preferred_element_type=jnp.float32
    )
    grad_w_key = jnp.einsum("td,ti->di", normed_one, grad_keys, preferred_element_type=jnp.float32)
    grad_w_value = jnp.einsum(
        "td,ti->di", normed_one, grad_values, preferred_element_type=jnp.float32
    )
    grad_normed_one = jnp.einsum(
        "ti,di->td", grad_queries, attn_set[1], preferred_element_type=jnp.float32
    )
    grad_normed_one = grad_normed_one + jnp.einsum(
        "ti,di->td", grad_keys, attn_set[2], preferred_element_type=jnp.float32
    )
    grad_normed_one = grad_normed_one + jnp.einsum(
        "ti,di->td", grad_values, attn_set[3], preferred_element_type=jnp.float32
    )
    rows_part, grad_gain_one = jax.vjp(norm_local, residual, gain_one)[1](grad_normed_one)
    grad_tokens = (grad_middle + rows_part).astype(jnp.bfloat16)
    grad_table = jnp.dot(grad_offsets, one_hot, precision=highest).T
    owner_start = lax.axis_index("shard") * owner_rows
    attn_shards = (
        lax.psum_scatter(grad_w_query.reshape(-1), "shard", scatter_dimension=0, tiled=True),
        lax.psum_scatter(grad_w_key.reshape(-1), "shard", scatter_dimension=0, tiled=True),
        lax.psum_scatter(grad_w_value.reshape(-1), "shard", scatter_dimension=0, tiled=True),
        lax.psum_scatter(grad_w_output.reshape(-1), "shard", scatter_dimension=0, tiled=True),
    )
    summed = lax.psum(
        (
            attn_shards[0],
            attn_shards[1],
            attn_shards[2],
            attn_shards[3],
            ffn_shards[0],
            ffn_shards[1],
            ffn_shards[2],
        ),
        "rep",
    )
    small_total = lax.psum((grad_gain_one, grad_gain_two, grad_table), ("shard", "rep"))
    gain_one_own = lax.dynamic_slice_in_dim(small_total[0], owner_start, owner_rows, 0)
    gain_two_own = lax.dynamic_slice_in_dim(small_total[1], owner_start, owner_rows, 0)
    return (
        layer_out,
        grad_tokens,
        gain_one_own,
        summed[0].reshape(owner_rows, inner_width),
        summed[1].reshape(owner_rows, inner_width),
        summed[2].reshape(owner_rows, inner_width),
        summed[3].reshape(owner_rows, inner_width),
        gain_two_own,
        summed[4].reshape(owner_rows, ff_width),
        summed[5].reshape(owner_rows, ff_width),
        summed[6].reshape(owner_rows, ff_width),
        small_total[2],
    )


def solution(mesh):
    return jax.shard_map(
        body,
        mesh=mesh,
        in_specs=(
            P(("shard", "rep"), None),
            P(("shard", "rep"), None),
            P(),
            P(),
            P("shard"),
            P("shard", None),
            P("shard", None),
            P("shard", None),
            P("shard", None),
            P("shard"),
            P("shard", None),
            P("shard", None),
            P("shard", None),
        ),
        out_specs=(
            P(("shard", "rep"), None),
            P(("shard", "rep"), None),
            P("shard"),
            P("shard", None),
            P("shard", None),
            P("shard", None),
            P("shard", None),
            P("shard"),
            P("shard", None),
            P("shard", None),
            P("shard", None),
            P(),
        ),
        check_vma=False,
    )
```

profile of v0, /device:TPU:1, one launch (start us, length us, event | category | flops | bytes accessed | tf_op | source)
XLA Modules:
  0.0 1683.8 jit_solution(12634931581973380931)
XLA Ops:
  14.1 12.9 all-reduce.13
  27.7 6.1 tile.24
  33.8 13.6 reshape.296
  47.5 14.0 tile.25
  61.5 11.4 slice.43
  72.9 13.1 reshape.298
  86.0 14.3 reshape.261
  100.3 6.8 slice.44
  107.1 6.9 copy.45
  114.6 2.2 convolution_convert_fusion.4
  116.9 2.4 convolution_convert_fusion.3
  119.3 2.4 convolution_convert_fusion.5
  121.7 4.9 fusion.48
  130.4 2.7 multiply_reduce_fusion.3
  135.4 43.5 %all-gather.18.cloned.1.call-done = bf16[1472,3584]{1,0:T(8,128)(2,1)} async-done(((bf16[184,3584]{1,0:T(8,128)(2,1)}), bf16[1472,3584]{1,0:T(8,128)(2,1)}) %all-gather.18.cloned.1.call-update) | async-done | bytes 10551312 | tf_op jit(solution)/shard_map/all_gather | solution.py:124
  178.9 11.0 fusion.50
  189.9 54.3 %all-gather.16.cloned.1.call-done = bf16[1472,3584]{1,0:T(8,128)(2,1)} async-done(((bf16[184,3584]{1,0:T(8,128)(2,1)}), bf16[1472,3584]{1,0:T(8,128)(2,1)}) %all-gather.16.cloned.1.call-update) | async-done | bytes 10551312 | tf_op jit(solution)/shard_map/all_gather | solution.py:123
  244.2 11.3 fusion.49
  255.6 54.1 %all-gather.20.cloned.1.call-done = bf16[1472,3584]{1,0:T(8,128)(2,1)} async-done(((bf16[184,3584]{1,0:T(8,128)(2,1)}), bf16[1472,3584]{1,0:T(8,128)(2,1)}) %all-gather.20.cloned.1.call-update) | async-done | bytes 10551312 | tf_op jit(solution)/shard_map/all_gather | solution.py:125
  309.7 19.0 %multiply_convert_fusion = (bf16[512,3584]{1,0:T(8,128)(2,1)S(1)}, bf16[512,3584]{1,0:T(8,128)(2,1)S(1)}, bf16[512,3584]{1,0:T(8,128)(2,1)}) fusion(f32[512,3584]{1,0:T(8,128)} %fusion.49, f32[512,3584]{1,0:T(8,128)} %fusion.50, bf16[512,1472]{0,1:T(8,128)(2,1)} %param.14, bf16[1472,3584]{1,0:T(8,128)(2,1)} %all-gather.20.cloned.1.call-done), kind=kOutput, calls=%fused_computation.11 | convolution fusion | flops 5449973760 | bytes 37748736 | tf_op jit(solution)/shard_map/dot_general | solution.py:143
  328.7 12.8 fusion.51
  341.5 10.9 multiply_reduce_fusion.1
  353.2 2.4 fusion.27
  358.9 1.9 multiply_convert_fusion.2
  360.8 1.8 convolution_convert_fusion
  364.0 10.1 fusion.53
  374.1 10.3 fusion.52
  384.5 3.0 reshape.269
  387.5 3.8 fusion.38
  391.3 3.0 reshape.267
  394.3 3.8 fusion.40
  398.1 3.1 reshape.265
  401.2 3.8 fusion.42
  405.0 3.1 reshape.263
  408.1 12.0 convolution_bitcast_fusion
  420.1 21.5 %reshape.275 = f32[5275648]{0:T(1024)} reshape(f32[1472,3584]{1,0:T(8,128)} %convolution_bitcast_fusion) | data formatting | bytes 42205184 | tf_op jit(solution)/shard_map/reshape | solution.py:159
  441.5 21.5 %reshape.273 = f32[5275648]{0:T(1024)} reshape(f32[1472,3584]{1,0:T(8,128)} %fusion.53) | data formatting | bytes 42205184 | tf_op jit(solution)/shard_map/reshape | solution.py:158
  463.0 21.5 %reshape.271 = f32[5275648]{0:T(1024)} reshape(f32[1472,3584]{1,0:T(8,128)} %fusion.52) | data formatting | bytes 42205184 | tf_op jit(solution)/shard_map/reshape | solution.py:157
  485.8 825.1 %all-reduce.17.cloned.1.call-done = (f32[565248]{0:T(1024)}, f32[565248]{0:T(1024)}, f32[565248]{0:T(1024)}, f32[565248]{0:T(1024)}, f32[5275648]{0:T(1024)}, /*index=5*/f32[5275648]{0:T(1024)}, f32[5275648]{0:T(1024)}) async-done(((f32[565248]{0:T(1024)}, f32[565248]{0:T(1024)}, f32[565248]{0:T(1024)}, f32[565248]{0:T(1024)}, f32[5275648]{0:T(1024)}, /*index=5*/f32[5275648]{0:T(1024)}, f32[5275648]{0:T(1024)}), ...) | async-done | bytes 72351760
  1312.6 1.7 reshape.264
  1316.0 1.7 reshape.266
  1321.1 1.7 reshape.270
  1322.9 1.7 reshape.268
  1324.6 3.4 dynamic-slice.11
  1328.0 3.9 reshape.272
  1331.9 3.4 dynamic-slice.13
  1335.3 3.4 dynamic-slice.15
  1338.7 3.5 reshape.276
  1342.3 3.5 reshape.274
  1345.8 31.4 %rev.8 = f32[6,512,512]{1,2,0:T(8,128)} reverse(bf16[6,512,512]{1,2,0:T(8,128)(2,1)S(1)} %multiply_convert_fusion.2), dimensions={2} | reverse | bytes 9437184 | tf_op jit(solution)/shard_map/while/body/eval_jaxpr/rev | solution.py:28
  1377.2 6.6 copy.46
  1383.8 9.2 pad_bitcast_fusion
  1393.0 18.0 %copy.47 = f32[1,6,512,1024]{3,1,2,0:T(8,128)} copy(f32[1,6,512,1024]{3,2,1,0:T(8,128)} %pad_bitcast_fusion) | data formatting | bytes 25165824
  1411.0 11.7 slice.45
  1422.7 12.2 reshape.300
  1435.0 14.1 reshape.278
  1449.1 5.6 reduce_sum.101
  1457.9 3.1 fusion.16
  1461.0 45.8 %all-reduce.10 = (f32[1472]{0:T(1024)S(1)}, f32[1472]{0:T(1024)S(1)}, f32[32,6]{0,1:T(8,128)}) all-reduce(f32[1472]{0:T(1024)S(1)} %get-tuple-element.62, f32[1472]{0:T(1024)S(1)} %copy-done.28, f32[32,6]{0,1:T(8,128)S(1)} %fusion.30), channel_id=1, replica_groups=mesh['shard'=8,'rep'=4] {'shard','rep'}, use_global_device_ids=true, to_apply=%region_8.9 | all-reduce | flops 3136 | bytes 25088 | tf_op jit(solution)/shard_map/psum | solution.py:250
  1508.1 4.8 fusion.19
  1513.8 9.2 fusion.22
  1523.0 139.5 %all-reduce.19.cloned.1.call-done = (f32[184,384]{1,0:T(8,128)}, f32[184,384]{1,0:T(8,128)}, f32[184,384]{1,0:T(8,128)}, f32[184,384]{1,0:T(8,128)}, f32[184,358...) async-done(((f32[184,384]{1,0:T(8,128)}, f32[184,384]{1,0:T(8,128)}, f32[184,384]{1,0:T(8,128)}, f32[184,384]{1,0:T(8,128)}, f32[184,3584]{1,0:T(8,128)}, ...) | async-done | bytes 9043984 | tf_op jit(solution)/shard_map/psum | solution.py:238
  1667.6 1.8 copy.67
  1669.5 3.4 copy.68
  (149 shorter events, 40.4 us)
Async XLA Ops:
  7.2 4.8 copy-start
  7.2 5.2 copy-start.29
  7.2 4.8 copy-start.30
  7.2 6.4 copy-start.32
  7.2 6.7 copy-start.33
  7.2 107.4 %all-gather.10.cloned.1.call-start = ((), (), s32[]{:S(2)}) async-start(), calls=%async_computation.1 | async-start | bytes 1271808 | tf_op jit(solution)/shard_map/all_gather | solution.py:73
  8.0 108.9 %all-gather.12.cloned.1.call-start = ((), (), s32[]{:S(2)}) async-start(), calls=%async_computation.2 | async-start | bytes 1271808 | tf_op jit(solution)/shard_map/all_gather | solution.py:74
  8.7 110.6 %all-gather.8.cloned.1.call-start = ((), (), s32[]{:S(2)}) async-start(), calls=%async_computation | async-start | bytes 1271808 | tf_op jit(solution)/shard_map/all_gather | solution.py:75
  9.5 121.0 %all-gather.14.cloned.1.call-start = ((), (), s32[]{:S(2)}) async-start(), calls=%async_computation.3 | async-start | bytes 1271808 | tf_op jit(solution)/shard_map/all_gather | solution.py:76
  10.0 168.9 %all-gather.18.cloned.1.call-start = ((), (), s32[]{:S(2)}) async-start(), calls=%async_computation.5 | async-start | bytes 11870208 | tf_op jit(solution)/shard_map/all_gather | solution.py:124
  10.6 233.6 %all-gather.16.cloned.1.call-start = ((), (), s32[]{:S(2)}) async-start(), calls=%async_computation.4 | async-start | bytes 11870208 | tf_op jit(solution)/shard_map/all_gather | solution.py:123
  11.2 298.5 %all-gather.20.cloned.1.call-start = ((), (), s32[]{:S(2)}) async-start(), calls=%async_computation.6 | async-start | bytes 11870208 | tf_op jit(solution)/shard_map/all_gather | solution.py:125
  11.9 1299.0 %all-reduce.17.cloned.1.call-start = ((), (), s32[]{:S(2)}) async-start(), calls=%async_computation.7 | async-start | bytes 144703488
  107.1 6.9 copy-start.7
  114.4 4.9 copy-start.26
  116.9 4.8 copy-start.14
  119.3 7.3 copy-start.16
  121.7 5.8 copy-start.23
  126.6 2.6 copy-start.2
  133.2 219.2 %copy-start.5 = (f32[512,1472]{0,1:T(8,128)}, f32[512,1472]{0,1:T(8,128)S(1)}, u32[]{:S(2)}) copy-start(f32[512,1472]{0,1:T(8,128)S(1)} %get-tuple-element.103) | copy-start | bytes 9043972
  328.6 12.8 copy-start.35
  328.6 12.8 copy-start.37
  328.6 27.7 %slice-start = ((s8[6291456]{0:T(1024)(128)(4,1)}), s8[4194304]{0:T(1024)(128)(4,1)S(1)}, s32[]{:S(2)}) async-start(s8[6291456]{0:T(1024)(128)(4,1)} %bitcast.72), calls=%async_computation.9 | async-start | bytes 8388608
  341.4 10.9 copy-start.19
  341.5 14.9 slice-start.1
  353.1 3.2 copy-start.3
  353.1 2.4 copy-start.9
  355.5 0.9 copy-start.25
  356.4 1.1 copy-start.24
  358.9 1.9 copy-start.15
  360.8 1.9 copy-start.17
  360.8 3.2 copy-start.18
  360.8 3.2 copy-start.38
  364.0 10.1 copy-start.36
  484.5 1178.1 %all-reduce.19.cloned.1.call-start = ((), (), s32[]{:S(2)}) async-start(), calls=%async_computation.8 | async-start | bytes 18087936 | tf_op jit(solution)/shard_map/psum | solution.py:238
  1449.1 5.7 copy-start.31
  1449.1 6.1 copy-start.13
  1449.1 6.1 copy-start.21
  1454.8 1.4 copy-start.12
  1454.8 1.4 copy-start.20
  1456.1 1.4 copy-start.8
  1456.2 1.7 copy-start.22
  1457.9 3.1 copy-start.28
  1457.9 50.1 %copy-start.27 = (f32[512]{0:T(512)S(1)}, f32[512]{0:T(512)}, u32[]{:S(2)}) copy-start(f32[512]{0:T(512)} %copy-done.26) | copy-start | bytes 6148
  1457.9 50.1 %copy-start.4 = (f32[512,1472]{0,1:T(8,128)S(1)}, f32[512,1472]{0,1:T(8,128)}, u32[]{:S(2)}) copy-start(f32[512,1472]{0,1:T(8,128)} %copy-done.3) | copy-start | bytes 9043972
  1508.0 4.8 copy-start.6
  1508.0 5.8 copy-start.34
  1667.6 5.3 copy-start.11
  1672.9 2.7 copy-start.10
  1672.9 4.2 copy-start.1
Sparse Core Ops, SparseCore 0:
  10.0 26.4 all-gather.9
  38.4 23.8 all-gather.11
  64.1 23.8 all-gather.7
  89.7 23.8 all-gather.13
  115.4 63.5 all-gather.17
  180.7 63.5 all-gather.15
  246.1 63.5 all-gather.19
  484.6 826.2 all-reduce.16
  1345.9 316.5 all-reduce.18
where the time goes:
time: 1700 us; the launch traced here: 1680 us
  waiting for transfers between devices  1120 us (66%)
  local copies, waits for them, and re-layouts  322 us (19%)
  matrix products  148 us (9%)
  blocking collectives  58.6 us (3%)
    unnamed x10, waiting for transfers between devices  829 us
    psum x1, waiting for transfers between devices, body(): lax.psum((attn_shards[0], attn_shards[1], attn_shards[2], attn_shards[3],...  140 us
    unnamed x110, local copies, waits for them, and re-layouts  116 us
    all_gather x1, waiting for transfers between devices, body(): lax.all_gather(w_gate, 'shard', axis=0, tiled=True)  54.3 us
    all_gather x1, waiting for transfers between devices, body(): lax.all_gather(w_down, 'shard', axis=0, tiled=True)  54.1 us
    psum x1, blocking collectives, body(): lax.psum((grad_gain_one, grad_gain_two, grad_table), ('shard', 'rep'))  45.8 us
    all_gather x1, waiting for transfers between devices, body(): lax.all_gather(w_up, 'shard', axis=0, tiled=True)  43.5 us
  transfers between devices with their start and end apart: 9, of which 5 were waited for; matrix products, arithmetic and copies ran while one was open for 15% of the time, Pallas kernels for 0%

commit v1 on v0

--- a/solution.py
+++ b/solution.py
@@ -154,9 +154,9 @@
     middle_part, grad_gain_two = jax.vjp(norm_local, middle, gain_two)[1](grad_normed_two)
     grad_middle = cotangent.astype(jnp.float32) + middle_part
     ffn_shards = (
-        lax.psum_scatter(grad_w_gate.reshape(-1), "shard", scatter_dimension=0, tiled=True),
-        lax.psum_scatter(grad_w_up.reshape(-1), "shard", scatter_dimension=0, tiled=True),
-        lax.psum_scatter(grad_w_down.reshape(-1), "shard", scatter_dimension=0, tiled=True),
+        lax.psum_scatter(grad_w_gate.astype(jnp.bfloat16), "shard", scatter_dimension=0, tiled=True),
+        lax.psum_scatter(grad_w_up.astype(jnp.bfloat16), "shard", scatter_dimension=0, tiled=True),
+        lax.psum_scatter(grad_w_down.astype(jnp.bfloat16), "shard", scatter_dimension=0, tiled=True),
     )
     attn_set = (
         lax.all_gather(attn_gain, "shard", axis=0, tiled=True),
@@ -230,10 +230,10 @@
     grad_table = jnp.dot(grad_offsets, one_hot, precision=highest).T
     owner_start = lax.axis_index("shard") * owner_rows
     attn_shards = (
-        lax.psum_scatter(grad_w_query.reshape(-1), "shard", scatter_dimension=0, tiled=True),
-        lax.psum_scatter(grad_w_key.reshape(-1), "shard", scatter_dimension=0, tiled=True),
-        lax.psum_scatter(grad_w_value.reshape(-1), "shard", scatter_dimension=0, tiled=True),
-        lax.psum_scatter(grad_w_output.reshape(-1), "shard", scatter_dimension=0, tiled=True),
+        lax.psum_scatter(grad_w_query.astype(jnp.bfloat16), "shard", scatter_dimension=0, tiled=True),
+        lax.psum_scatter(grad_w_key.astype(jnp.bfloat16), "shard", scatter_dimension=0, tiled=True),
+        lax.psum_scatter(grad_w_value.astype(jnp.bfloat16), "shard", scatter_dimension=0, tiled=True),
+        lax.psum_scatter(grad_w_output.astype(jnp.bfloat16), "shard", scatter_dimension=0, tiled=True),
     )
     summed = lax.psum(
         (
@@ -254,14 +254,14 @@
         layer_out,
         grad_tokens,
         gain_one_own,
-        summed[0].reshape(owner_rows, inner_width),
-        summed[1].reshape(owner_rows, inner_width),
-        summed[2].reshape(owner_rows, inner_width),
-        summed[3].reshape(owner_rows, inner_width),
+        summed[0].astype(jnp.float32),
+        summed[1].astype(jnp.float32),
+        summed[2].astype(jnp.float32),
+        summed[3].astype(jnp.float32),
         gain_two_own,
-        summed[4].reshape(owner_rows, ff_width),
-        summed[5].reshape(owner_rows, ff_width),
-        summed[6].reshape(owner_rows, ff_width),
+        summed[4].astype(jnp.float32),
+        summed[5].astype(jnp.float32),
+        summed[6].astype(jnp.float32),
         small_total[2],
     )
 

time: 1700 us -> 973 us (0.57)
  waiting for transfers between devices: 1120 us -> 513 us
  local copies, waits for them, and re-layouts: 322 us -> 197 us
  other arithmetic: 16.7 us -> 33.7 us
    unnamed x10 -> x19, waiting for transfers between devices: 829 us -> 104 us
    reduce_scatter x0 -> x3, waiting for transfers between devices: none -> 256 us  [the longest x1 85.4 us: body(): lax.psum_scatter(grad_w_up.astype(jnp.bfloat16), 'shard', scatter_dimensi...]
    psum x1, waiting for transfers between devices: 140 us -> 0.01 us  [body(): lax.psum((attn_shards[0], attn_shards[1], attn_shards[2], attn_shards[3],...]
    reshape x14 -> x0, local copies, waits for them, and re-layouts: 94.4 us -> none  [the longest x1 21.5 us: body(): grad_w_gate.reshape(-1)]
    unnamed x110 -> x90, local copies, waits for them, and re-layouts: 116 us -> 85.1 us
  transfers between devices with their start and end apart: 9 -> 15, of which waited for: 5 -> 9; matrix products, arithmetic and copies ran while one was open for 15% -> 33% of each run, Pallas kernels for 0% -> 0%
where the time goes in v1:
time: 973 us; the launch traced here: 962 us
  waiting for transfers between devices  513 us (53%)
  local copies, waits for them, and re-layouts  197 us (20%)
  matrix products  145 us (15%)
  blocking collectives  56.4 us (6%)
  other arithmetic  33.7 us (3%)
  between operations  15.7 us (2%)
    unnamed x19, waiting for transfers between devices  104 us
    reduce_scatter x1, waiting for transfers between devices, body(): lax.psum_scatter(grad_w_up.astype(jnp.bfloat16), 'shard', scatter_dimensi...  85.4 us
    reduce_scatter x1, waiting for transfers between devices, body(): lax.psum_scatter(grad_w_down.astype(jnp.bfloat16), 'shard', scatter_dimen...  85.4 us
    reduce_scatter x1, waiting for transfers between devices, body(): lax.psum_scatter(grad_w_gate.astype(jnp.bfloat16), 'shard', scatter_dimen...  85.3 us
    unnamed x90, local copies, waits for them, and re-layouts  85.1 us
    all_gather x1, waiting for transfers between devices, body(): lax.all_gather(w_gate, 'shard', axis=0, tiled=True)  54.4 us
    all_gather x1, waiting for transfers between devices, body(): lax.all_gather(w_down, 'shard', axis=0, tiled=True)  54.3 us
    all_gather x1, waiting for transfers between devices, body(): lax.all_gather(w_up, 'shard', axis=0, tiled=True)  44.1 us
  transfers between devices with their start and end apart: 15, of which 9 were waited for; matrix products, arithmetic and copies ran while one was open for 33% of the time, Pallas kernels for 0%

profile of v1, /device:TPU:1, one launch (start us, length us, event | category | flops | bytes accessed | tf_op | source)
XLA Modules:
  0.0 961.6 jit_solution(3687832752011226338)
XLA Ops:
  14.1 12.9 %all-reduce.8 = (bf16[1472]{0:T(1024)(128)(2,1)S(1)}, bf16[1472]{0:T(1024)(128)(2,1)S(1)}) all-reduce(bf16[1472]{0:T(1024)(128)(2,1)S(1)} %dynamic-update-slice, bf16[1472]{0:T(1024)(128)(2,1)S(1)} %dynamic-update-slice.1), channel_id=1, replica_groups=mesh['shard'=8,'rep'=4] {'shard'}, use_global_device_ids=true, to_apply=%add.1 | all-reduce | flops 2944 | bytes 11776
  27.7 6.1 tile.24
  33.8 13.6 %reshape.237 = f32[3142656]{0:T(1024)} reshape(f32[6,512,1023]{2,1,0:T(8,128)} %tile.24) | data formatting | bytes 25141248
  47.4 14.0 %tile.25 = f32[6,523776]{1,0:T(8,128)} reshape(f32[3142656]{0:T(1024)} %reshape.237) | data formatting | bytes 25141248 | tf_op jit(solution)/shard_map/while/body/eval_jaxpr/tile | solution.py:42
  61.4 11.4 %slice.43 = f32[6,523264]{1,0:T(8,128)} slice(f32[6,523776]{1,0:T(8,128)} %tile.25), slice={[0:6], [0:523264]} | slice | bytes 25116672 | tf_op jit(solution)/shard_map/while/body/eval_jaxpr/slice | solution.py:42
  72.9 13.1 %reshape.239 = f32[3139584]{0:T(1024)} reshape(f32[6,523264]{1,0:T(8,128)} %slice.43) | data formatting | bytes 25116672
  86.0 14.2 %reshape.219 = f32[6,512,1022]{2,1,0:T(8,128)} reshape(f32[3139584]{0:T(1024)} %reshape.239) | data formatting | bytes 25116672 | tf_op jit(solution)/shard_map/while/body/eval_jaxpr/reshape | solution.py:43
  100.2 6.8 slice.44
  107.0 6.8 copy.45
  114.5 2.2 convolution_convert_fusion.11
  116.8 2.4 convolution_convert_fusion.10
  119.2 2.4 convolution_convert_fusion.12
  121.6 4.9 fusion.44
  127.4 1.7 copy-done.2
  129.1 1.2 fusion.27
  130.3 2.7 multiply_reduce_fusion.3
  133.1 1.8 multiply_convert_fusion.3
  134.9 44.1 %all-gather.18.cloned.1.call-done = bf16[1472,3584]{1,0:T(8,128)(2,1)} async-done(((bf16[184,3584]{1,0:T(8,128)(2,1)}), bf16[1472,3584]{1,0:T(8,128)(2,1)}) %all-gather.18.cloned.1.call-update) | async-done | bytes 10551312 | tf_op jit(solution)/shard_map/all_gather | solution.py:124
  178.9 10.9 %fusion.46 = f32[512,3584]{1,0:T(8,128)} fusion(bf16[512,1472]{0,1:T(8,128)(2,1)} %multiply_convert_fusion.3, bf16[1472,3584]{1,0:T(8,128)(2,1)} %all-gather.18.cloned.1.call-done), kind=kOutput, calls=%fused_computation.90 | convolution fusion | flops 5402263552 | bytes 19398656 | tf_op jit(solution)/shard_map/dot_general | solution.py:130
  189.9 54.4 %all-gather.16.cloned.1.call-done = bf16[1472,3584]{1,0:T(8,128)(2,1)} async-done(((bf16[184,3584]{1,0:T(8,128)(2,1)}), bf16[1472,3584]{1,0:T(8,128)(2,1)}) %all-gather.16.cloned.1.call-update) | async-done | bytes 10551312 | tf_op jit(solution)/shard_map/all_gather | solution.py:123
  244.2 11.2 %fusion.45 = f32[512,3584]{1,0:T(8,128)} fusion(bf16[512,1472]{0,1:T(8,128)(2,1)} %multiply_convert_fusion.3, bf16[1472,3584]{1,0:T(8,128)(2,1)} %all-gather.16.cloned.1.call-done), kind=kOutput, calls=%fused_computation.89 | convolution fusion | flops 5402263552 | bytes 19398656 | tf_op jit(solution)/shard_map/dot_general | solution.py:129
  255.4 54.3 %all-gather.20.cloned.1.call-done = bf16[1472,3584]{1,0:T(8,128)(2,1)} async-done(((bf16[184,3584]{1,0:T(8,128)(2,1)}), bf16[1472,3584]{1,0:T(8,128)(2,1)}) %all-gather.20.cloned.1.call-update) | async-done | bytes 10551312 | tf_op jit(solution)/shard_map/all_gather | solution.py:125
  309.7 19.0 %multiply_convert_fusion = (bf16[512,3584]{1,0:T(8,128)(2,1)S(1)}, bf16[512,3584]{1,0:T(8,128)(2,1)S(1)}, bf16[512,3584]{1,0:T(8,128)(2,1)}) fusion(f32[512,3584]{1,0:T(8,128)} %fusion.45, f32[512,3584]{1,0:T(8,128)} %fusion.46, bf16[512,1472]{0,1:T(8,128)(2,1)} %param.14, bf16[1472,3584]{1,0:T(8,128)(2,1)} %all-gather.20.cloned.1.call-done), kind=kOutput, calls=%fused_computation.14 | convolution fusion | flops 5449973760 | bytes 37748736 | tf_op jit(solution)/shard_map/dot_general | solution.py:143
  328.7 11.0 %fusion.47 = f32[512,1472]{0,1:T(8,128)S(1)} fusion(bf16[512,3584]{1,0:T(8,128)(2,1)S(1)} %get-tuple-element.89, bf16[1472,3584]{1,0:T(8,128)(2,1)} %all-gather.16.cloned.1.call-done), kind=kOutput, calls=%fused_computation.91 | convolution fusion | flops 5402263552 | bytes 17235968 | tf_op jit(solution)/shard_map/tf,df->td/dot_general | solution.py:148
  339.8 10.6 %multiply_reduce_fusion.1 = (f32[1472]{0:T(1024)}, f32[512]{0:T(512)S(1)}, f32[512,1472]{0,1:T(8,128)S(1)}) fusion(f32[512,1472]{0,1:T(8,128)S(1)} %get-tuple-element.94, f32[512]{0:T(512)S(1)} %fusion.37, f32[1472]{0:T(1024)S(1)} %convert_element_type.157, f32[512,1472]{0,1:T(8,128)S(1)} %fusion.47, bf16[512,3584]{1,0:T(8,128)(2,1)S(1)} %get-tuple-element.88, ...), kind=kOutput, calls=%fused_computation.48 | convolution fusion | flops 5407537152 | bytes 23281152 | tf_op jit(solution)/shard_map/tf,df->td/dot_general | solution.py:151
  350.3 2.7 fusion.18
  353.1 2.0 convolution_convert_fusion.3
  355.1 2.1 convolution_convert_fusion.9
  357.3 4.0 fusion.24
  362.1 2.0 convolution_convert_fusion.4
  364.1 4.4 multiply_reduce_fusion
  368.5 4.1 multiply_convert_fusion.2
  374.1 2.0 convolution_convert_fusion.6
  376.2 2.2 convolution_convert_fusion.7
  378.4 2.0 convolution_convert_fusion.5
  380.4 10.4 %fusion = bf16[1472,3584]{1,0:T(8,128)(2,1)} fusion(bf16[512,1472]{0,1:T(8,128)(2,1)} %param.14, bf16[512,3584]{1,0:T(8,128)(2,1)} %get-tuple-element.90), kind=kOutput, calls=%fused_computation.3 | convolution fusion | flops 5407539200 | bytes 15728640 | tf_op jit(solution)/shard_map/td,tf->df/dot_general | solution.py:142
  390.9 10.1 %convolution_convert_fusion.1 = bf16[1472,3584]{1,0:T(8,128)(2,1)} fusion(bf16[512,1472]{0,1:T(8,128)(2,1)} %multiply_convert_fusion.3, bf16[512,3584]{1,0:T(8,128)(2,1)} %copy-done.37), kind=kOutput, calls=%fused_computation.1 | convolution fusion | flops 5407539200 | bytes 15728640 | tf_op jit(solution)/shard_map/td,tf->df/dot_general | solution.py:147
  401.1 10.3 %convolution_convert_fusion.2 = bf16[1472,3584]{1,0:T(8,128)(2,1)} fusion(bf16[512,1472]{0,1:T(8,128)(2,1)} %multiply_convert_fusion.3, bf16[512,3584]{1,0:T(8,128)(2,1)} %copy-done.36), kind=kOutput, calls=%fused_computation.2 | convolution fusion | flops 5407539200 | bytes 15728640 | tf_op jit(solution)/shard_map/td,tf->df/dot_general | solution.py:146
  411.5 19.7 %reduce-scatter.26.cloned.1.call-done = bf16[184,384]{1,0:T(8,128)(2,1)} async-done(((bf16[1472,384]{1,0:T(8,128)(2,1)}), bf16[184,384]{1,0:T(8,128)(2,1)}) %reduce-scatter.26.cloned.1.call-update) | async-done | bytes 141328
  431.1 39.9 %reduce-scatter.22.cloned.1.call-done = bf16[184,384]{1,0:T(8,128)(2,1)} async-done(((bf16[1472,384]{1,0:T(8,128)(2,1)}), bf16[184,384]{1,0:T(8,128)(2,1)}) %reduce-scatter.22.cloned.1.call-update) | async-done | bytes 141328
  471.1 40.1 %reduce-scatter.24.cloned.1.call-done = bf16[184,384]{1,0:T(8,128)(2,1)} async-done(((bf16[1472,384]{1,0:T(8,128)(2,1)}), bf16[184,384]{1,0:T(8,128)(2,1)}) %reduce-scatter.24.cloned.1.call-update) | async-done | bytes 141328
  511.1 85.4 %reduce-scatter.20.cloned.1.call-done = bf16[184,3584]{1,0:T(8,128)(2,1)} async-done(((bf16[1472,3584]{1,0:T(8,128)(2,1)}), bf16[184,3584]{1,0:T(8,128)(2,1)}) %reduce-scatter.20.cloned.1.call-update) | async-done | bytes 1318928 | tf_op jit(solution)/shard_map/reduce_scatter | solution.py:159
  596.5 85.4 %reduce-scatter.18.cloned.1.call-done = bf16[184,3584]{1,0:T(8,128)(2,1)} async-done(((bf16[1472,3584]{1,0:T(8,128)(2,1)}), bf16[184,3584]{1,0:T(8,128)(2,1)}) %reduce-scatter.18.cloned.1.call-update) | async-done | bytes 1318928 | tf_op jit(solution)/shard_map/reduce_scatter | solution.py:158
  681.9 85.3 %reduce-scatter.16.cloned.1.call-done = bf16[184,3584]{1,0:T(8,128)(2,1)} async-done(((bf16[1472,3584]{1,0:T(8,128)(2,1)}), bf16[184,3584]{1,0:T(8,128)(2,1)}) %reduce-scatter.16.cloned.1.call-update) | async-done | bytes 1318928 | tf_op jit(solution)/shard_map/reduce_scatter | solution.py:157
  767.3 31.7 %rev.8 = f32[6,512,512]{1,2,0:T(8,128)} reverse(bf16[6,512,512]{1,2,0:T(8,128)(2,1)S(1)} %multiply_convert_fusion.2), dimensions={2} | reverse | bytes 9437184 | tf_op jit(solution)/shard_map/while/body/eval_jaxpr/rev | solution.py:28
  799.0 6.5 copy.46
  805.5 9.3 pad_bitcast_fusion
  814.7 17.9 %copy.47 = f32[1,6,512,1024]{3,1,2,0:T(8,128)} copy(f32[1,6,512,1024]{3,2,1,0:T(8,128)} %pad_bitcast_fusion) | data formatting | bytes 25165824
  832.6 11.5 %slice.45 = f32[6,523776]{1,0:T(8,128)} slice(f32[6,524288]{1,0:T(8,128)} %bitcast.72), slice={[0:6], [0:523776]} | slice | bytes 25141248 | tf_op jit(solution)/shard_map/while/body/eval_jaxpr/slice | solution.py:33
  844.1 12.2 %reshape.241 = f32[3142656]{0:T(1024)} reshape(f32[6,523776]{1,0:T(8,128)} %slice.45) | data formatting | bytes 25141248
  856.3 14.4 %reshape.222 = f32[6,512,1023]{2,1,0:T(8,128)} reshape(f32[3142656]{0:T(1024)} %reshape.241) | data formatting | bytes 25141248 | tf_op jit(solution)/shard_map/while/body/eval_jaxpr/reshape | solution.py:34
  870.7 5.7 reduce_sum.101
  877.9 1.0 convolution_add_fusion.1
  879.7 3.0 fusion.17
  882.7 43.5 %all-reduce.7 = (f32[1472]{0:T(1024)S(1)}, f32[1472]{0:T(1024)S(1)}, f32[32,6]{0,1:T(8,128)}) all-reduce(f32[1472]{0:T(1024)S(1)} %get-tuple-element.62, f32[1472]{0:T(1024)S(1)} %copy-done.29, f32[32,6]{0,1:T(8,128)S(1)} %fusion.30), channel_id=1, replica_groups=mesh['shard'=8,'rep'=4] {'shard','rep'}, use_global_device_ids=true, to_apply=%region_8.9 | all-reduce | flops 3136 | bytes 25088 | tf_op jit(solution)/shard_map/psum | solution.py:250
  927.6 4.4 fusion.20
  932.0 9.2 fusion.23
  941.2 1.7 convert_element_type.179
  943.0 1.6 convert_element_type.181
  944.6 1.6 convert_element_type.183
  946.2 1.6 convert_element_type.185
  947.9 3.2 convert_element_type.187
  951.1 1.8 convert_element_type.189
  952.9 1.8 convert_element_type.192
  (139 shorter events, 14.5 us)
Async XLA Ops:
  7.2 4.8 copy-start
  7.2 5.2 copy-start.34
  7.2 4.8 copy-start.30
  7.2 6.4 copy-start.32
  7.2 6.6 copy-start.33
  7.2 107.3 %all-gather.10.cloned.1.call-start = ((), (), s32[]{:S(2)}) async-start(), calls=%async_computation.8 | async-start | bytes 1271808 | tf_op jit(solution)/shard_map/all_gather | solution.py:73
  8.0 108.8 %all-gather.12.cloned.1.call-start = ((), (), s32[]{:S(2)}) async-start(), calls=%async_computation.9 | async-start | bytes 1271808 | tf_op jit(solution)/shard_map/all_gather | solution.py:74
  8.7 110.5 %all-gather.8.cloned.1.call-start = ((), (), s32[]{:S(2)}) async-start(), calls=%async_computation.7 | async-start | bytes 1271808 | tf_op jit(solution)/shard_map/all_gather | solution.py:75
  9.5 120.9 %all-gather.14.cloned.1.call-start = ((), (), s32[]{:S(2)}) async-start(), calls=%async_computation.10 | async-start | bytes 1271808 | tf_op jit(solution)/shard_map/all_gather | solution.py:76
  10.0 168.9 %all-gather.18.cloned.1.call-start = ((), (), s32[]{:S(2)}) async-start(), calls=%async_computation.12 | async-start | bytes 11870208 | tf_op jit(solution)/shard_map/all_gather | solution.py:124
  10.6 233.6 %all-gather.16.cloned.1.call-start = ((), (), s32[]{:S(2)}) async-start(), calls=%async_computation.11 | async-start | bytes 11870208 | tf_op jit(solution)/shard_map/all_gather | solution.py:123
  11.2 298.5 %all-gather.20.cloned.1.call-start = ((), (), s32[]{:S(2)}) async-start(), calls=%async_computation.13 | async-start | bytes 11870208 | tf_op jit(solution)/shard_map/all_gather | solution.py:125
  11.9 399.5 %reduce-scatter.28.cloned.1.call-start = ((), (), s32[]{:S(2)}) async-start(), calls=%async_computation.20 | async-start | bytes 1271808
  107.0 6.9 copy-start.7
  114.2 4.9 copy-start.27
  116.7 4.8 copy-start.16
  119.2 7.3 copy-start.17
  121.6 5.8 copy-start.25
  126.5 2.6 copy-start.2
  133.1 206.6 %copy-start.5 = (f32[512,1472]{0,1:T(8,128)}, f32[512,1472]{0,1:T(8,128)S(1)}, u32[]{:S(2)}) copy-start(f32[512,1472]{0,1:T(8,128)S(1)} %get-tuple-element.94) | copy-start | bytes 9043972
  328.7 11.0 %copy-start.36 = (bf16[512,3584]{1,0:T(8,128)(2,1)}, bf16[512,3584]{1,0:T(8,128)(2,1)S(1)}, u32[]{:S(2)}) copy-start(bf16[512,3584]{1,0:T(8,128)(2,1)S(1)} %get-tuple-element.89) | copy-start | bytes 11010052
  328.7 11.0 %copy-start.37 = (bf16[512,3584]{1,0:T(8,128)(2,1)}, bf16[512,3584]{1,0:T(8,128)(2,1)S(1)}, u32[]{:S(2)}) copy-start(bf16[512,3584]{1,0:T(8,128)(2,1)S(1)} %get-tuple-element.88) | copy-start | bytes 11010052
  339.7 10.6 %copy-start.19 = (bf16[512,1472]{0,1:T(8,128)(2,1)S(1)}, bf16[512,1472]{0,1:T(8,128)(2,1)}, u32[]{:S(2)}) copy-start(bf16[512,1472]{0,1:T(8,128)(2,1)} %param.14) | copy-start | bytes 4521988
  353.1 4.2 copy-start.3
  355.1 76.0 %reduce-scatter.26.cloned.1.call-start = ((), (), s32[]{:S(2)}) async-start(), calls=%async_computation.19 | async-start | bytes 1271808
  357.2 4.8 copy-start.8
  361.3 0.8 copy-start.12
  361.3 2.8 copy-start.26
  364.1 107.0 %reduce-scatter.22.cloned.1.call-start = ((), (), s32[]{:S(2)}) async-start(), calls=%async_computation.17 | async-start | bytes 1271808
  368.5 4.1 copy-start.18
  372.7 1.4 copy-start.9
  373.3 0.8 copy-start.14
  376.1 135.0 %reduce-scatter.24.cloned.1.call-start = ((), (), s32[]{:S(2)}) async-start(), calls=%async_computation.18 | async-start | bytes 1271808
  376.2 2.2 copy-start.10
  380.4 216.1 %reduce-scatter.20.cloned.1.call-start = ((), (), s32[]{:S(2)}) async-start(), calls=%async_computation.16 | async-start | bytes 11870208 | tf_op jit(solution)/shard_map/reduce_scatter | solution.py:159
  390.8 291.1 %reduce-scatter.18.cloned.1.call-start = ((), (), s32[]{:S(2)}) async-start(), calls=%async_computation.15 | async-start | bytes 11870208 | tf_op jit(solution)/shard_map/reduce_scatter | solution.py:158
  401.0 366.2 %reduce-scatter.16.cloned.1.call-start = ((), (), s32[]{:S(2)}) async-start(), calls=%async_computation.14 | async-start | bytes 11870208 | tf_op jit(solution)/shard_map/reduce_scatter | solution.py:157
  411.4 529.8 %all-reduce.12.cloned.1.call-start = ((), (), s32[]{:S(2)}) async-start(), calls=%async_computation.21 | async-start | bytes 9043968 | tf_op jit(solution)/shard_map/psum | solution.py:238
  870.7 5.7 copy-start.31
  870.7 6.1 copy-start.15
  870.7 6.1 copy-start.23
  876.4 1.4 copy-start.22
  877.8 1.4 copy-start.11
  877.8 1.4 copy-start.13
  877.8 1.8 copy-start.24
  879.7 3.1 copy-start.29
  879.7 47.9 %copy-start.28 = (f32[512]{0:T(512)S(1)}, f32[512]{0:T(512)}, u32[]{:S(2)}) copy-start(f32[512]{0:T(512)} %copy-done.27) | copy-start | bytes 6148
  879.7 47.9 %copy-start.4 = (f32[512,1472]{0,1:T(8,128)S(1)}, f32[512,1472]{0,1:T(8,128)}, u32[]{:S(2)}) copy-start(f32[512,1472]{0,1:T(8,128)} %copy-done.3) | copy-start | bytes 9043972
  927.5 4.4 copy-start.6
  927.6 4.4 copy-start.35
  941.2 9.9 %copy-start.21 = (bf16[184,3584]{1,0:T(8,128)(2,1)S(1)}, bf16[184,3584]{1,0:T(8,128)(2,1)}, u32[]{:S(2)}) copy-start(bf16[184,3584]{1,0:T(8,128)(2,1)} %get-tuple-element.86) | copy-start | bytes 3956740
  947.9 5.0 copy-start.20
  951.1 3.6 copy-start.1
Sparse Core Ops, SparseCore 0:
  10.0 26.4 all-gather.9
  38.4 23.8 all-gather.11
  64.1 23.8 all-gather.7
  89.7 23.8 all-gather.13
  115.4 63.5 all-gather.17
  180.7 63.5 all-gather.15
  246.1 63.5 all-gather.19
  355.2 35.7 reduce-scatter.27
  394.9 36.1 reduce-scatter.25
  434.8 36.1 reduce-scatter.21
  474.9 36.1 reduce-scatter.23
  514.5 81.9 reduce-scatter.19
  600.0 81.8 reduce-scatter.17
  685.3 81.8 reduce-scatter.15
  770.0 168.7 all-reduce.11
